TPU v7x, 512 devices: a whole 4x8x8 slice. The times are simulated.
512 devices in a mesh: section: 8 (over y), tensor: 32 (over x_hi, z, core), dp: 2 (over x_lo).
Axes of the slice: x: 4 (x_hi: 2, x_lo: 2; x = x_hi * 2 + x_lo), y: 8, z: 8, core: 2. Of those that a mesh axis runs over, the one named last changes fastest.
Arguments:
- acts: bfloat16 [8, 2, 256, 3328], P('section', None, ('tensor', 'dp')), may hold values from -6 to 6
- cotangent: bfloat16 [8, 2, 256, 3328], P('section', None, ('tensor', 'dp')), may hold values from -6 to 6
- w_in: bfloat16 [8, 3328, 8960], P('section', 'dp', 'tensor'), may hold values from -0.109375 to 0.109375
- w_out: bfloat16 [8, 8960, 3328], P('section', 'tensor', 'dp'), may hold values from -0.0625 to 0.0625
Outputs:
- result: bfloat16 [8, 2, 256, 3328], P('section', None, ('tensor', 'dp'))
- d_acts: bfloat16 [8, 2, 256, 3328], P('section', None, ('tensor', 'dp'))
- grad_in: bfloat16 [8, 3328, 8960], P('section', 'dp', 'tensor')
- grad_out: bfloat16 [8, 8960, 3328], P('section', 'tensor', 'dp')
All inputs are finite; a program needn't handle non-finite values.
Results may differ from a plain program's by a relative error of at most 0.015.
Values may be sent and summed in bfloat16 or wider, within the bound.
A program may use at most 64 MiB of HBM per device.

v0:
```python
import jax
import jax.numpy as jnp
from jax import lax
from jax.sharding import PartitionSpec as P


def from_partner(block, axis, bit):
    count = lax.axis_size(axis)
    route = []
    for low in range(count):
        high = low | 1 << bit
        if high != low and high < count:
            route += [(low, high), (high, low)]
    return lax.ppermute(block, axis, route)


def mirror(first, second):
    for bit in range(lax.axis_size("section").bit_length() - 1):
        first, second = from_partner((first, second), "section", bit)
    return (first, second)


def inner_rows(left, right):
    return lax.dot_general(
        left, right, (((0,), (0,)), ((), ())), preferred_element_type=jnp.float32
    )


def inner_cols(left, right):
    return lax.dot_general(
        left, right, (((1,), (1,)), ((), ())), preferred_element_type=jnp.float32
    )


def on_device(acts, cotangent, w_in, w_out):
    tok = acts.shape[2]
    far_x, far_g = mirror(acts[0, 1][None], cotangent[0, 1][None])
    rows = jnp.concatenate([acts[0, 0], far_x[0]], 0)
    grads = jnp.concatenate([cotangent[0, 0], far_g[0]], 0)
    full_in, full_out = (
        lax.all_gather(w_in, "dp", axis=1, tiled=True),
        lax.all_gather(w_out, "dp", axis=2, tiled=True),
    )
    weight_one = full_in[0]
    weight_two = full_out[0]
    gathered = lax.all_gather(rows, "tensor", axis=0, tiled=True)
    hidden = jnp.dot(gathered, weight_one, preferred_element_type=jnp.float32)
    act, gelu_back = jax.vjp(jax.nn.gelu, hidden)
    act_b = act.astype(jnp.bfloat16)
    piece = act_b
    branch = lax.psum_scatter(
        jnp.dot(piece, weight_two, preferred_element_type=jnp.float32).astype(jnp.bfloat16),
        "tensor",
        scatter_dimension=0,
        tiled=True,
    ).astype(jnp.float32)
    outputs = (rows.astype(jnp.float32) + branch).astype(jnp.bfloat16)
    grad_all = lax.all_gather(grads, "tensor", axis=0, tiled=True)
    d_act = inner_cols(grad_all, weight_two)
    d_hid = gelu_back(d_act)[0].astype(jnp.bfloat16)
    piece = d_hid
    back = lax.psum_scatter(
        inner_cols(piece, weight_one).astype(jnp.bfloat16),
        "tensor",
        scatter_dimension=0,
        tiled=True,
    ).astype(jnp.float32)
    d_rows = (grads.astype(jnp.float32) + back).astype(jnp.bfloat16)
    half = w_in.shape[1]
    side = lax.axis_index("dp")
    other = 1 - side
    whole_in = inner_rows(gathered, d_hid)
    whole_out = inner_rows(act_b, grad_all)
    part_in, part_out = (
        from_partner(
            lax.dynamic_slice_in_dim(whole_in, other * half, half, 0).astype(jnp.bfloat16), "dp", 0
        ).astype(jnp.float32),
        from_partner(
            lax.dynamic_slice_in_dim(whole_out, other * half, half, 1).astype(jnp.bfloat16), "dp", 0
        ).astype(jnp.float32),
    )
    g_in = lax.dynamic_slice_in_dim(whole_in, side * half, half, 0) + part_in
    g_out = lax.dynamic_slice_in_dim(whole_out, side * half, half, 1) + part_out
    back_y, back_dx = mirror(outputs[tok:][None], d_rows[tok:][None])
    result = jnp.stack([outputs[:tok], back_y[0]], 0)[None]
    d_acts = jnp.stack([d_rows[:tok], back_dx[0]], 0)[None]
    return (result, d_acts, g_in.astype(jnp.bfloat16)[None], g_out.astype(jnp.bfloat16)[None])


def solution(mesh):
    placed = (
        P("section", None, ("tensor", "dp"), None),
        P("section", None, ("tensor", "dp"), None),
        P("section", "dp", "tensor"),
        P("section", "tensor", "dp"),
    )
    return jax.shard_map(
        on_device,
        mesh=mesh,
        in_specs=placed,
        out_specs=(
            P("section", None, ("tensor", "dp"), None),
            P("section", None, ("tensor", "dp"), None),
            P("section", "dp", "tensor"),
            P("section", "tensor", "dp"),
        ),
        check_vma=False,
    )
```

profile of v0, /device:TPU:2, one launch (start us, length us, event | category | flops | bytes accessed | tf_op | source)
XLA Modules:
  0.0 562.4 jit_solution(723908907127146015)
XLA Ops:
  7.2 0.7 all-gather.7.cloned.1.call-update
  8.0 0.8 slice_bitcast_fusion.7
  8.7 3.5 collective-permute-start
  12.2 2.2 collective-permute-done
  14.5 4.5 collective-permute-start.1
  19.0 2.1 collective-permute-done.1
  21.1 8.0 %collective-permute-start.2 = (bf16[1,4,3328]{2,1,0:T(4,128)(2,1)S(1)}, bf16[1,4,3328]{2,1,0:T(4,128)(2,1)S(1)}, u32[]{:S(2)}, u32[]{:S(2)}) collective-permute-start(bf16[1,4,3328]{2,1,0:T(4,128)(2,1)S(1)} %collective-permute-done.1), channel_id=1, source_target_pairs={{0,256},{256,0},{64,320},{320,64},{128,384},{384,128},{192,448},{4... | collective-permute-start | bytes 79880 | tf_op jit(solution)/shard_map/ppermute | solution.py:14
  29.1 2.1 collective-permute-done.2
  31.2 0.7 pad_maximum_fusion
  31.9 0.0 all-gather.9.cloned.1.call-start
  32.0 0.7 all-gather.9.cloned.1.call-update
  32.7 3.1 collective-permute-start.6
  35.8 2.7 collective-permute-done.6
  38.5 4.1 collective-permute-start.7
  42.6 2.5 collective-permute-done.7
  45.1 7.5 %collective-permute-start.8 = (bf16[1,4,3328]{2,1,0:T(4,128)(2,1)S(1)}, bf16[1,4,3328]{2,1,0:T(4,128)(2,1)S(1)}, u32[]{:S(2)}, u32[]{:S(2)}) collective-permute-start(bf16[1,4,3328]{2,1,0:T(4,128)(2,1)S(1)} %collective-permute-done.7), channel_id=1, source_target_pairs={{0,256},{256,0},{64,320},{320,64},{128,384},{384,128},{192,448},{4... | collective-permute-start | bytes 79880 | tf_op jit(solution)/shard_map/ppermute | solution.py:14
  52.6 2.2 collective-permute-done.8
  54.8 0.7 pad_maximum_fusion.1
  55.5 0.0 reduce-scatter.3.cloned.1.call-start
  55.6 86.6 %all-gather.5.cloned.1.call-done = bf16[256,3328]{1,0:T(8,128)(2,1)} async-done(((bf16[8,3328]{1,0:T(8,128)(2,1)}), bf16[256,3328]{1,0:T(8,128)(2,1)}) %all-gather.5.cloned.1.call-update) | async-done | bytes 1703952 | tf_op jit(solution)/shard_map/all_gather | solution.py:46
  142.2 2.7 fusion.4
  144.9 33.6 %all-gather.9.cloned.1.call-done = bf16[1,280,3328]{2,1,0:T(8,128)(2,1)} async-done(((bf16[1,280,1664]{2,1,0:T(8,128)(2,1)}), bf16[1,280,3328]{2,1,0:T(8,128)(2,1)}) %all-gather.9.cloned.1.call-update) | async-done | bytes 1863696 | tf_op jit(solution)/shard_map/all_gather | solution.py:42
  178.5 4.0 convolution_convert_fusion.1
  182.7 86.0 %all-gather.11.cloned.1.call-done = bf16[256,3328]{1,0:T(8,128)(2,1)} async-done(((bf16[8,3328]{1,0:T(8,128)(2,1)}), bf16[256,3328]{1,0:T(8,128)(2,1)}) %all-gather.11.cloned.1.call-update) | async-done | bytes 1703952 | tf_op jit(solution)/shard_map/all_gather | solution.py:58
  268.6 2.4 fusion.14
  271.0 2.3 convolution_convert_fusion
  273.4 0.7 fusion.18
  274.0 1.0 dynamic-slice_convert_fusion.1
  275.1 3.5 collective-permute-start.12
  278.6 0.7 fusion.17
  279.3 0.1 dynamic-slice_convert_fusion
  279.4 1.7 copy-done.1
  281.1 2.5 collective-permute-start.13
  283.6 111.5 %reduce-scatter.3.cloned.1.call-done = bf16[8,3328]{1,0:T(8,128)(2,1)} async-done(((bf16[256,3328]{1,0:T(8,128)(2,1)}), bf16[8,3328]{1,0:T(8,128)(2,1)}) %reduce-scatter.3.cloned.1.call-update) | async-done | bytes 53264 | tf_op jit(solution)/shard_map/reduce_scatter | solution.py:51
  395.1 0.8 add_convert_fusion.3
  396.0 3.4 collective-permute-start.3
  399.4 124.3 %reduce-scatter.5.cloned.1.call-done = bf16[8,3328]{1,0:T(8,128)(2,1)} async-done(((bf16[256,3328]{1,0:T(8,128)(2,1)}), bf16[8,3328]{1,0:T(8,128)(2,1)}) %reduce-scatter.5.cloned.1.call-update) | async-done | bytes 53264 | tf_op jit(solution)/shard_map/reduce_scatter | solution.py:62
  523.7 0.8 add_convert_fusion.2
  524.6 3.7 collective-permute-start.9
  528.3 4.3 collective-permute-start.4
  532.6 2.6 fusion.6
  535.2 2.4 collective-permute-start.10
  537.7 6.5 %collective-permute-start.5 = (bf16[1,4,3328]{2,1,0:T(4,128)(2,1)S(1)}, bf16[1,4,3328]{2,1,0:T(4,128)(2,1)S(1)}, u32[]{:S(2)}, u32[]{:S(2)}) collective-permute-start(bf16[1,4,3328]{2,1,0:T(4,128)(2,1)S(1)} %collective-permute-done.4), channel_id=1, source_target_pairs={{0,256},{256,0},{64,320},{320,64},{128,384},{384,128},{192,448},{4... | collective-permute-start | bytes 79880 | tf_op jit(solution)/shard_map/ppermute | solution.py:14
  544.2 1.1 fusion.7
  545.3 3.3 collective-permute-start.11
  548.6 0.7 maximum_bitcast_fusion
  549.2 5.7 %collective-permute-done.11 = bf16[1,4,3328]{2,1,0:T(4,128)(2,1)S(1)} collective-permute-done((bf16[1,4,3328]{2,1,0:T(4,128)(2,1)S(1)}, bf16[1,4,3328]{2,1,0:T(4,128)(2,1)S(1)}, u32[]{:S(2)}, u32[]{:S(2)}) %collective-permute-start.11) | collective-permute-done | bytes 26656 | tf_op jit(solution)/shard_map/ppermute | solution.py:14
  554.9 0.7 maximum_bitcast_fusion.1
  (34 shorter events, 0.4 us)
Async XLA Ops:
  7.2 25.5 %copy-start.7 = (bf16[1,2,4,3328]{3,2,1,0:T(4,128)(2,1)S(1)}, bf16[1,2,4,3328]{3,2,1,0:T(4,128)(2,1)}, u32[]{:S(2)}) copy-start(bf16[1,2,4,3328]{3,2,1,0:T(4,128)(2,1)} %param.5) | copy-start | bytes 159748
  7.2 48.4 %all-gather.7.cloned.1.call-start = ((), (), s32[]{:S(2)}) async-start(), calls=%async_computation.3 | async-start | bytes 2795520 | tf_op jit(solution)/shard_map/all_gather | solution.py:41
  7.9 134.3 %all-gather.5.cloned.1.call-start = ((), (), s32[]{:S(2)}) async-start(), calls=%async_computation.2 | async-start | bytes 1757184 | tf_op jit(solution)/shard_map/all_gather | solution.py:46
  8.7 5.7 %collective-permute-start = (bf16[1,4,3328]{2,1,0:T(4,128)(2,1)S(1)}, bf16[1,4,3328]{2,1,0:T(4,128)(2,1)S(1)}, u32[]{:S(2)}, u32[]{:S(2)}) collective-permute-start(bf16[1,4,3328]{2,1,0:T(4,128)(2,1)S(1)} %get-tuple-element.11), channel_id=1, source_target_pairs={{0,64},{64,0},{128,192},{192,128},{256,320},{320,256},{384,448},{4... | collective-permute-start | bytes 79880 | tf_op jit(solution)/shard_map/ppermute | solution.py:14
  14.5 6.6 %collective-permute-start.1 = (bf16[1,4,3328]{2,1,0:T(4,128)(2,1)S(1)}, bf16[1,4,3328]{2,1,0:T(4,128)(2,1)S(1)}, u32[]{:S(2)}, u32[]{:S(2)}) collective-permute-start(bf16[1,4,3328]{2,1,0:T(4,128)(2,1)S(1)} %collective-permute-done), channel_id=1, source_target_pairs={{0,128},{128,0},{64,192},{192,64},{256,384},{384,256},{320,448},{4... | collective-permute-start | bytes 79880 | tf_op jit(solution)/shard_map/ppermute | solution.py:14
  21.1 10.1 %collective-permute-start.2 = (bf16[1,4,3328]{2,1,0:T(4,128)(2,1)S(1)}, bf16[1,4,3328]{2,1,0:T(4,128)(2,1)S(1)}, u32[]{:S(2)}, u32[]{:S(2)}) collective-permute-start(bf16[1,4,3328]{2,1,0:T(4,128)(2,1)S(1)} %collective-permute-done.1), channel_id=1, source_target_pairs={{0,256},{256,0},{64,320},{320,64},{128,384},{384,128},{192,448},{4... | collective-permute-start | bytes 79880 | tf_op jit(solution)/shard_map/ppermute | solution.py:14
  31.9 146.6 %all-gather.9.cloned.1.call-start = ((), (), s32[]{:S(2)}) async-start(), calls=%async_computation.4 | async-start | bytes 2795520 | tf_op jit(solution)/shard_map/all_gather | solution.py:42
  32.6 236.0 %all-gather.11.cloned.1.call-start = ((), (), s32[]{:S(2)}) async-start(), calls=%async_computation.6 | async-start | bytes 1757184 | tf_op jit(solution)/shard_map/all_gather | solution.py:58
  32.7 5.7 %collective-permute-start.6 = (bf16[1,4,3328]{2,1,0:T(4,128)(2,1)S(1)}, bf16[1,4,3328]{2,1,0:T(4,128)(2,1)S(1)}, u32[]{:S(2)}, u32[]{:S(2)}) collective-permute-start(bf16[1,4,3328]{2,1,0:T(4,128)(2,1)S(1)} %get-tuple-element.7), channel_id=1, source_target_pairs={{0,64},{64,0},{128,192},{192,128},{256,320},{320,256},{384,448},{4... | collective-permute-start | bytes 79880 | tf_op jit(solution)/shard_map/ppermute | solution.py:14
  38.5 6.6 %collective-permute-start.7 = (bf16[1,4,3328]{2,1,0:T(4,128)(2,1)S(1)}, bf16[1,4,3328]{2,1,0:T(4,128)(2,1)S(1)}, u32[]{:S(2)}, u32[]{:S(2)}) collective-permute-start(bf16[1,4,3328]{2,1,0:T(4,128)(2,1)S(1)} %collective-permute-done.6), channel_id=1, source_target_pairs={{0,128},{128,0},{64,192},{192,64},{256,384},{384,256},{320,448},{4... | collective-permute-start | bytes 79880 | tf_op jit(solution)/shard_map/ppermute | solution.py:14
  45.1 9.7 %collective-permute-start.8 = (bf16[1,4,3328]{2,1,0:T(4,128)(2,1)S(1)}, bf16[1,4,3328]{2,1,0:T(4,128)(2,1)S(1)}, u32[]{:S(2)}, u32[]{:S(2)}) collective-permute-start(bf16[1,4,3328]{2,1,0:T(4,128)(2,1)S(1)} %collective-permute-done.7), channel_id=1, source_target_pairs={{0,256},{256,0},{64,320},{320,64},{128,384},{384,128},{192,448},{4... | collective-permute-start | bytes 79880 | tf_op jit(solution)/shard_map/ppermute | solution.py:14
  55.5 339.6 %reduce-scatter.3.cloned.1.call-start = ((), (), s32[]{:S(2)}) async-start(), calls=%async_computation.5 | async-start | bytes 1757184 | tf_op jit(solution)/shard_map/reduce_scatter | solution.py:51
  178.5 90.1 %copy-start.5 = (bf16[1,280,3328]{2,1,0:T(8,128)(2,1)S(1)}, bf16[1,280,3328]{2,1,0:T(8,128)(2,1)}, u32[]{:S(2)}) copy-start(bf16[1,280,3328]{2,1,0:T(8,128)(2,1)} %all-gather.9.cloned.1.call-done) | copy-start | bytes 5591044
  182.6 341.1 %reduce-scatter.5.cloned.1.call-start = ((), (), s32[]{:S(2)}) async-start(), calls=%async_computation.7 | async-start | bytes 1757184 | tf_op jit(solution)/shard_map/reduce_scatter | solution.py:62
  268.6 2.4 copy-start.4
  271.0 2.3 copy-start.3
  274.0 5.3 copy-start
  274.0 4.5 copy-start.6
  275.1 257.5 %collective-permute-start.12 = (bf16[1664,280]{0,1:T(8,128)(2,1)}, bf16[1664,280]{0,1:T(8,128)(2,1)S(1)}, u32[]{:S(2)}, u32[]{:S(2)}) collective-permute-start(bf16[1664,280]{0,1:T(8,128)(2,1)} %dynamic-slice_convert_fusion.1), channel_id=1, source_target_pairs={{0,1},{1,0},{2,3},{3,2},{4,5},{5,4},{6,7},{7,6},{8,9},{9,8},{10,11... | collective-permute-start | bytes 2795528 | tf_op jit(solution)/shard_map/ppermute | solution.py:14
  279.3 1.8 copy-start.1
  281.1 263.0 %collective-permute-start.13 = (bf16[280,1664]{1,0:T(8,128)(2,1)S(1)}, bf16[280,1664]{1,0:T(8,128)(2,1)S(1)}, u32[]{:S(2)}, u32[]{:S(2)}) collective-permute-start(bf16[280,1664]{1,0:T(8,128)(2,1)S(1)} %dynamic-slice_convert_fusion), channel_id=1, source_target_pairs={{0,1},{1,0},{2,3},{3,2},{4,5},{5,4},{6,7},{7,6},{8,9},{9,8},{10,11... | collective-permute-start | bytes 2795528 | tf_op jit(solution)/shard_map/ppermute | solution.py:14
  396.0 132.3 %collective-permute-start.3 = (bf16[1,4,3328]{2,1,0:T(4,128)(2,1)S(1)}, bf16[1,4,3328]{2,1,0:T(4,128)(2,1)S(1)}, u32[]{:S(2)}, u32[]{:S(2)}) collective-permute-start(bf16[1,4,3328]{2,1,0:T(4,128)(2,1)S(1)} %get-tuple-element.9), channel_id=1, source_target_pairs={{0,64},{64,0},{128,192},{192,128},{256,320},{320,256},{384,448},{4... | collective-permute-start | bytes 79880 | tf_op jit(solution)/shard_map/ppermute | solution.py:14
  524.6 19.6 %copy-start.2 = (f32[280,3328]{1,0:T(8,128)S(1)}, f32[280,3328]{1,0:T(8,128)}, u32[]{:S(2)}) copy-start(f32[280,3328]{1,0:T(8,128)} %copy-done.1) | copy-start | bytes 11182084
  524.6 10.6 %collective-permute-start.9 = (bf16[1,4,3328]{2,1,0:T(4,128)(2,1)S(1)}, bf16[1,4,3328]{2,1,0:T(4,128)(2,1)S(1)}, u32[]{:S(2)}, u32[]{:S(2)}) collective-permute-start(bf16[1,4,3328]{2,1,0:T(4,128)(2,1)S(1)} %get-tuple-element.5), channel_id=1, source_target_pairs={{0,64},{64,0},{128,192},{192,128},{256,320},{320,256},{384,448},{4... | collective-permute-start | bytes 79880 | tf_op jit(solution)/shard_map/ppermute | solution.py:14
  528.3 9.4 %collective-permute-start.4 = (bf16[1,4,3328]{2,1,0:T(4,128)(2,1)S(1)}, bf16[1,4,3328]{2,1,0:T(4,128)(2,1)S(1)}, u32[]{:S(2)}, u32[]{:S(2)}) collective-permute-start(bf16[1,4,3328]{2,1,0:T(4,128)(2,1)S(1)} %collective-permute-done.3), channel_id=1, source_target_pairs={{0,128},{128,0},{64,192},{192,64},{256,384},{384,256},{320,448},{4... | collective-permute-start | bytes 79880 | tf_op jit(solution)/shard_map/ppermute | solution.py:14
  535.2 10.0 %collective-permute-start.10 = (bf16[1,4,3328]{2,1,0:T(4,128)(2,1)S(1)}, bf16[1,4,3328]{2,1,0:T(4,128)(2,1)S(1)}, u32[]{:S(2)}, u32[]{:S(2)}) collective-permute-start(bf16[1,4,3328]{2,1,0:T(4,128)(2,1)S(1)} %collective-permute-done.9), channel_id=1, source_target_pairs={{0,128},{128,0},{64,192},{192,64},{256,384},{384,256},{320,448},{4... | collective-permute-start | bytes 79880 | tf_op jit(solution)/shard_map/ppermute | solution.py:14
  537.7 10.9 %collective-permute-start.5 = (bf16[1,4,3328]{2,1,0:T(4,128)(2,1)S(1)}, bf16[1,4,3328]{2,1,0:T(4,128)(2,1)S(1)}, u32[]{:S(2)}, u32[]{:S(2)}) collective-permute-start(bf16[1,4,3328]{2,1,0:T(4,128)(2,1)S(1)} %collective-permute-done.4), channel_id=1, source_target_pairs={{0,256},{256,0},{64,320},{320,64},{128,384},{384,128},{192,448},{4... | collective-permute-start | bytes 79880 | tf_op jit(solution)/shard_map/ppermute | solution.py:14
  545.3 9.6 %collective-permute-start.11 = (bf16[1,4,3328]{2,1,0:T(4,128)(2,1)S(1)}, bf16[1,4,3328]{2,1,0:T(4,128)(2,1)S(1)}, u32[]{:S(2)}, u32[]{:S(2)}) collective-permute-start(bf16[1,4,3328]{2,1,0:T(4,128)(2,1)S(1)} %collective-permute-done.10), channel_id=1, source_target_pairs={{0,256},{256,0},{64,320},{320,64},{128,384},{384,128},{192,448},{4... | collective-permute-start | bytes 79880 | tf_op jit(solution)/shard_map/ppermute | solution.py:14
Sparse Core Ops, SparseCore 0:
  10.1 41.8 all-gather.6
  55.8 86.3 all-gather.4
  144.3 34.1 all-gather.8
  182.2 86.3 all-gather.10
  273.2 121.8 reduce-scatter.2
  400.4 123.3 reduce-scatter.4
where the time goes:
time: 564 us; the launch traced here: 562 us
  waiting for transfers between devices  463 us (82%)
  starting transfers between devices  60.5 us (11%)
  between operations  14.4 us (3%)
  matrix products  12.8 us (2%)
  other arithmetic  8.04 us (1%)
    reduce_scatter x1, waiting for transfers between devices, on_device(): lax.psum_scatter(inner_cols(piece, weight_one).astype(jnp.bfloat16), 'ten...  124 us
    reduce_scatter x1, waiting for transfers between devices, on_device(): lax.psum_scatter(jnp.dot(piece, weight_two, preferred_element_type=jnp.fl...  112 us
    all_gather x1, waiting for transfers between devices, on_device(): gathered = lax.all_gather(rows, 'tensor', axis=0, tiled=True)  86.6 us
    all_gather x1, waiting for transfers between devices, on_device(): grad_all = lax.all_gather(grads, 'tensor', axis=0, tiled=True)  86 us
    ppermute x14, starting transfers between devices, from_partner(): return lax.ppermute(block, axis, route)  60.2 us
    all_gather x1, waiting for transfers between devices, on_device(): lax.all_gather(w_out, 'dp', axis=2, tiled=True)  33.6 us
    ppermute x14, waiting for transfers between devices, from_partner(): return lax.ppermute(block, axis, route)  19.5 us
  transfers between devices with their start and end apart: 20, of which 12 were waited for; matrix products, arithmetic and copies ran while one was open for 4% of the time, Pallas kernels for 0%

commit v1 on v0

v1 whole, which is shorter than its diff:
```python
import jax
import jax.numpy as jnp
from jax import lax
from jax.experimental import pallas as pl
from jax.experimental.pallas import tpu as pltpu
from jax.sharding import PartitionSpec as P

MESH = pl.DeviceIdType.MESH
BF, F32 = jnp.bfloat16, jnp.float32
RING = 8
HOPS = RING // 2
BLOCK = 32
GROUP = 4 * BLOCK
HALF = 2 * BLOCK
COPIES = 80
ROOT = 0.7978845608028654
CUBE = 0.044715


def nt(a, b):
    return lax.dot_general(a, b, (((1,), (1,)), ((), ())), preferred_element_type=F32)


def nn(a, b):
    return lax.dot_general(a, b, (((1,), (0,)), ((), ())), preferred_element_type=F32)


def tn(a, b):
    return lax.dot_general(a, b, (((0,), (0,)), ((), ())), preferred_element_type=F32)


def kernel(
    x_in, c_in, w1_hbm, w2_hbm,
    res, dx, gi_hbm, go_hbm,
    xs, xr, cs, cr, ys, yr, ds, dr, wide, X, C, w1, w2, gi, go,
    h_own, h_out, h_in, e_own, e_out, e_in, slope, act, grd,
    po, ps, pr, sp, rp, px, pxr, qo, qs, qr, sq, rq, qx, qxr,
    send_sem, recv_sem, local_sem,
):
    s, t, p = (lax.axis_index(a) for a in ("section", "tensor", "dp"))
    sections = lax.axis_size("section")
    core = t % 2
    z = (t // 2) % RING
    x_hi = t // (2 * RING)
    turn = 1 - 2 * core

    def at_z(step):
        return (s, x_hi * 2 * RING + ((z + RING + step) % RING) * 2 + core, p)

    up, down = at_z(turn), at_z(-turn)
    sib = (s, t + turn, p)
    across = (s, (t + 2 * RING) % (4 * RING), p)
    pair = (s, t, 1 - p)
    far = (sections - 1 - s, t, p)
    far_pair = (sections - 1 - s, t, 1 - p)
    half = w1.shape[1]

    barrier = pltpu.get_barrier_semaphore()
    peers = (up, down, sib, across, pair, far, far_pair)
    for peer in peers:
        pl.semaphore_signal(barrier, inc=1, device_id=peer, device_id_type=MESH)

    load1 = pltpu.make_async_copy(w1_hbm, w1, local_sem.at[0])
    load2 = pltpu.make_async_copy(w2_hbm, w2, local_sem.at[1])
    load1.start()
    load2.start()

    sent = []
    count = [0]

    def ticket():
        count[0] += 1
        return count[0] - 1

    def send(src, dst, device, n):
        copy = pltpu.make_async_remote_copy(
            src_ref=src, dst_ref=dst, send_sem=send_sem.at[n], recv_sem=recv_sem.at[n],
            device_id=device, device_id_type=MESH,
        )
        copy.start()
        sent.append(copy)

    def arrived(dst, device, n):
        pltpu.make_async_remote_copy(
            src_ref=dst, dst_ref=dst, send_sem=send_sem.at[n], recv_sem=recv_sem.at[n],
            device_id=device, device_id_type=MESH,
        ).wait_recv()

    for source, stage in ((x_in, xs), (c_in, cs)):
        for d in range(2):
            for h in range(2):
                stage[d, h] = source[d, :, h * half : (h + 1) * half]
    pl.semaphore_wait(barrier, len(peers))

    routes = ((0, 1, pair), (1, 0, far), (1, 1, far_pair))

    def spread(stage, land):
        numbers = [ticket() for _ in routes]
        for n, (d, rel, device) in zip(numbers, routes):
            other = p + rel - 2 * rel * p
            send(stage.at[d, other], land.at[d, p], device, n)
        land[0, p] = stage[0, p]
        return numbers

    def landed(land, numbers):
        for n, (d, rel, device) in zip(numbers, routes):
            arrived(land.at[d, p + rel - 2 * rel * p], device, n)

    x_spread = spread(xs, xr)
    c_spread = spread(cs, cr)

    ZERO = 13 * BLOCK

    def rows(ref, at, n):
        return ref.at[pl.ds(at, n)]

    def own_rows(land, numbers, buf):
        landed(land, numbers)
        for d in range(2):
            for q in range(2):
                at = (d * 2 + q) * 4
                wide[at : at + 4, :] = land[d, q].astype(F32)
        buf[ZERO : ZERO + 16, :] = wide[...].astype(BF)
        n = ticket()
        send(rows(buf, ZERO, 16), rows(buf, ZERO + 16, 16), across, n)
        return n

    class Gather:
        def __init__(self, buf):
            self.buf = buf
            self.a = [ticket() for _ in range(HOPS)]
            self.b = [ticket() for _ in range(HOPS - 1)]
            self.s = [ticket() for _ in range(HOPS + 1)]

        def place(self, k, which):
            if k == 0:
                return rows(self.buf, ZERO, BLOCK)
            return rows(self.buf, GROUP * (k - 1) + BLOCK * which, BLOCK)

        def start(self, n):
            arrived(rows(self.buf, ZERO + 16, 16), across, n)
            self.forward(0)
            send(self.place(0, 0), rows(self.buf, ZERO + HALF, BLOCK), sib, self.s[HOPS])

        def forward(self, k):
            if k < HOPS:
                send(self.place(k, 0), self.place(k + 1, 0), up, self.a[k])
            if k < HOPS - 1:
                send(self.place(k, 1), self.place(k + 1, 1), down, self.b[k])

        def step(self, k):
            arrived(self.place(k, 0), up, self.a[k - 1])
            if k < HOPS:
                arrived(self.place(k, 1), down, self.b[k - 1])
            self.forward(k)
            at, n = GROUP * (k - 1), HALF if k < HOPS else BLOCK
            send(rows(self.buf, at, n), rows(self.buf, at + HALF, n), sib, self.s[k - 1])

        def group(self, k):
            at, n = GROUP * (k - 1) + HALF, HALF if k < HOPS else BLOCK
            arrived(rows(self.buf, at, n), sib, self.s[k - 1])
            if k == HOPS:
                arrived(rows(self.buf, ZERO + HALF, BLOCK), sib, self.s[HOPS])

    class Inner:
        def __init__(self, gather, weight, own, out, inn):
            self.gather, self.weight = gather, weight
            self.own, self.out, self.inn = own, out, inn
            self.n = [ticket() for _ in range(HOPS)]

        def make(self, k):
            self.gather.group(k)
            at = GROUP * (k - 1)
            part = nt(self.gather.buf[at : at + GROUP, :], self.weight[...])
            self.own[at : at + GROUP, :] = part
            self.out[at : at + GROUP, :] = part.astype(BF)
            send(rows(self.out, at, GROUP), rows(self.inn, at, GROUP), pair, self.n[k - 1])

        def total(self, k):
            at = GROUP * (k - 1)
            arrived(rows(self.inn, at, GROUP), pair, self.n[k - 1])
            return self.own[at : at + GROUP, :] + self.inn[at : at + GROUP, :].astype(F32)

    class Scatter:
        def __init__(self, left, weight, own, out, inn, go_on, come, edge, edge_in, base, stage, land, dest):
            self.left, self.weight = left, weight
            self.own, self.out, self.inn = own, out, inn
            self.go_on, self.come = go_on, come
            self.edge, self.edge_in, self.base = edge, edge_in, base
            self.stage, self.land, self.dest = stage, land, dest
            self.s = [ticket() for _ in range(HOPS)]
            self.a = [ticket() for _ in range(HOPS)]
            self.b = [ticket() for _ in range(HOPS - 1)]
            self.x = ticket()

        def make(self, k):
            at = GROUP * (k - 1)
            term = nn(self.left[at : at + GROUP, :], self.weight[...])
            to = HALF * (k - 1)
            self.out[to : to + HALF, :] = term[HALF:, :].astype(BF)
            send(rows(self.out, to, HALF), rows(self.inn, to, HALF), sib, self.s[k - 1])
            self.own[to : to + HALF, :] = term[:HALF, :]

        def sums(self, at, n):
            return self.own[at : at + n, :] + self.inn[at : at + n, :].astype(F32)

        def step(self, k):
            to = HALF * (k - 1)
            arrived(rows(self.inn, to, HALF), sib, self.s[k - 1])
            if k < HOPS:
                arrived(rows(self.come, to + HALF, BLOCK), down, self.a[k])
            first = self.sums(to, BLOCK)
            if k < HOPS:
                first += self.come[to + HALF : to + HALF + BLOCK, :].astype(F32)
            self.go_on[to : to + BLOCK, :] = first.astype(BF)
            send(rows(self.go_on, to, BLOCK), rows(self.come, to, BLOCK), down, self.a[k - 1])
            if k < HOPS:
                mid = to + BLOCK
                second = self.sums(mid, BLOCK)
                if k < HOPS - 1:
                    arrived(rows(self.come, mid + HALF, BLOCK), up, self.b[k])
                    second += self.come[mid + HALF : mid + HALF + BLOCK, :].astype(F32)
                self.go_on[mid : mid + BLOCK, :] = second.astype(BF)
                send(rows(self.go_on, mid, BLOCK), rows(self.come, mid, BLOCK), up, self.b[k - 1])

        def edges(self):
            arrived(rows(self.come, 0, BLOCK), down, self.a[0])
            arrived(rows(self.come, BLOCK, BLOCK), up, self.b[0])
            at = HALF * HOPS - BLOCK
            all_here = self.sums(at, BLOCK) + self.come[0:BLOCK, :].astype(F32)
            all_here += self.come[BLOCK:HALF, :].astype(F32)
            self.edge[...] = all_here[16:, :].astype(BF)
            send(self.edge, self.edge_in, across, self.x)
            self.own[at : at + 16, :] = all_here[:16, :]

        def finish(self):
            arrived(self.edge_in, across, self.x)
            at = HALF * HOPS - BLOCK
            wide[...] = (
                self.own[at : at + 16, :]
                + self.edge_in[...].astype(F32)
                + self.base[ZERO : ZERO + 16, :].astype(F32)
            )
            for d in range(2):
                for q in range(2):
                    start = (d * 2 + q) * 4
                    self.stage[d, q] = wide[start : start + 4, :].astype(BF)
            self.numbers = spread(self.stage, self.land)

        def deliver(self):
            landed(self.land, self.numbers)
            for d in range(2):
                for h in range(2):
                    self.dest[d, :, h * half : (h + 1) * half] = self.land[d, h]

    def bend(k):
        at = GROUP * (k - 1)
        v = hid.total(k)
        square = v * v
        th = jnp.tanh(ROOT * (v + CUBE * (square * v)))
        gate = 0.5 * (1.0 + th)
        act[at : at + GROUP, :] = (v * gate).astype(BF)
        slope[at : at + GROUP, :] = gate + 0.5 * v * (1.0 - th * th) * (
            ROOT * (1.0 + 3.0 * CUBE * square)
        )

    def back(k):
        at = GROUP * (k - 1)
        grd[at : at + GROUP, :] = (err.total(k) * slope[at : at + GROUP, :]).astype(BF)

    gx, gc = Gather(X), Gather(C)
    hid = Inner(gx, w1, h_own, h_out, h_in)
    err = Inner(gc, w2, e_own, e_out, e_in)

    nx = own_rows(xr, x_spread, X)
    nc = own_rows(cr, c_spread, C)
    gx.start(nx)
    load1.wait()
    load2.wait()
    gx.step(1)
    gc.start(nc)
    gx.step(2)
    gc.step(1)
    hid.make(1)
    gx.step(3)
    gc.step(2)
    hid.make(2)
    gx.step(4)
    gc.step(3)
    hid.make(3)
    hid.make(4)
    err.make(1)
    err.make(2)
    bend(1)
    bend(2)
    bend(3)
    gc.step(4)
    err.make(3)

    sc_p = Scatter(act, w2, po, ps, pr, sp, rp, px, pxr, X, ys, yr, res)
    sc_q = Scatter(grd, w1, qo, qs, qr, sq, rq, qx, qxr, C, ds, dr, dx)

    bend(4)
    sc_p.make(4)
    sc_p.make(3)
    err.make(4)
    sc_p.step(4)
    sc_p.make(2)
    sc_p.make(1)
    back(1)
    back(2)
    back(3)
    sc_p.step(3)
    back(4)
    sc_q.make(4)
    sc_q.make(3)
    sc_q.step(4)
    sc_p.step(2)
    sc_q.make(2)
    sc_q.make(1)
    sc_q.step(3)
    go[...] = tn(act[...], C[...]).astype(BF)
    store1 = pltpu.make_async_copy(go, go_hbm, local_sem.at[2])
    store1.start()
    sc_p.step(1)
    sc_q.step(2)
    gi[...] = tn(grd[...], X[...]).astype(BF)
    store2 = pltpu.make_async_copy(gi, gi_hbm, local_sem.at[3])
    store2.start()
    sc_p.edges()
    sc_q.step(1)
    sc_p.finish()
    sc_q.edges()
    sc_q.finish()
    sc_p.deliver()
    sc_q.deliver()
    for copy in sent:
        copy.wait_send()
    store1.wait()
    store2.wait()


def on_device(acts, cotangent, w_in, w_out):
    _, hidden, half = w_out.shape
    d_model = 2 * half
    every = HOPS * GROUP
    v = pltpu.VMEM
    stage = v((2, 2, 4, half), BF)
    inner = [v((every, hidden), F32), v((every, hidden), BF), v((every, hidden), BF)]
    own = HALF * HOPS
    outer = [v((own, half), F32)] + [v((own, half), BF)] * 4 + [v((16, half), BF)] * 2
    any_place = pl.BlockSpec(memory_space=pl.ANY)
    here = pl.BlockSpec(memory_space=pltpu.VMEM)
    result, d_acts, g_in, g_out = pl.pallas_call(
        kernel,
        out_shape=(
            jax.ShapeDtypeStruct((2, 4, d_model), BF),
            jax.ShapeDtypeStruct((2, 4, d_model), BF),
            jax.ShapeDtypeStruct((hidden, half), BF),
            jax.ShapeDtypeStruct((hidden, half), BF),
        ),
        in_specs=[here, here, any_place, any_place],
        out_specs=(here, here, any_place, any_place),
        scratch_shapes=[stage] * 8
        + [v((16, half), F32)]
        + [v((every, half), BF)] * 2
        + [v((hidden, half), BF)] * 4
        + inner * 2
        + [v((every, hidden), F32), v((every, hidden), BF), v((every, hidden), BF)]
        + outer * 2
        + [
            pltpu.SemaphoreType.DMA((COPIES,)),
            pltpu.SemaphoreType.DMA((COPIES,)),
            pltpu.SemaphoreType.DMA((4,)),
        ],
        compiler_params=pltpu.CompilerParams(
            collective_id=0, has_side_effects=True, vmem_limit_bytes=48 * 1024 * 1024
        ),
        cost_estimate=pl.CostEstimate(
            flops=12 * every * hidden * half, bytes_accessed=8 * hidden * half, transcendentals=every * hidden
        ),
    )(acts[0], cotangent[0], jnp.swapaxes(w_in[0], 0, 1), w_out[0])
    return (result[None], d_acts[None], jnp.swapaxes(g_in, 0, 1)[None], g_out[None])


def solution(mesh):
    placed = (
        P("section", None, ("tensor", "dp"), None),
        P("section", None, ("tensor", "dp"), None),
        P("section", "dp", "tensor"),
        P("section", "tensor", "dp"),
    )
    return jax.shard_map(on_device, mesh=mesh, in_specs=placed, out_specs=placed, check_vma=False)
```

time: 564 us -> 95.3 us (0.17)
  the two profiles are of different devices: /device:TPU:2 before, /device:TPU:10 now
where the time goes in v1:
time: 95.3 us; the launch traced here: 95 us
  Pallas kernels  87.2 us (92%)
  local copies, waits for them, and re-layouts  7.08 us (7%)
    pallas_call x1, Pallas kernels, on_device(): pl.pallas_call(kernel, out_shape=(jax.ShapeDtypeStruct((2, 4, d_model), B...  87.2 us
    unnamed x12, local copies, waits for them, and re-layouts  7.08 us

profile of v1, /device:TPU:10, one launch (start us, length us, event | category | flops | bytes accessed | tf_op | source)
XLA Modules:
  0.0 95.0 jit_solution(1158639470994734946)
XLA Ops:
  0.6 0.0 copy-start
  0.6 1.2 %copy-done = bf16[1,1664,280]{1,2,0:T(8,128)(2,1)S(1)} copy-done((bf16[1,1664,280]{1,2,0:T(8,128)(2,1)S(1)}, bf16[1,1664,280]{1,2,0:T(8,128)(2,1)}, u32[]{:S(2)}) %copy-start) | copy-done | bytes 931864
  1.8 0.0 copy-start.1
  1.8 1.2 %copy-done.1 = bf16[1,280,1664]{2,1,0:T(8,128)(2,1)S(1)} copy-done((bf16[1,280,1664]{2,1,0:T(8,128)(2,1)S(1)}, bf16[1,280,1664]{2,1,0:T(8,128)(2,1)}, u32[]{:S(2)}) %copy-start.1) | copy-done | bytes 931864
  3.0 0.0 copy-start.2
  3.0 0.8 copy-done.2
  3.8 0.0 copy-start.3
  3.8 0.8 copy-done.3
  4.6 87.2 %shard_map.75 = (bf16[2,4,3328]{2,1,0:T(4,128)(2,1)S(1)}, bf16[2,4,3328]{2,1,0:T(4,128)(2,1)S(1)}, bf16[280,1664]{1,0:T(8,128)(2,1)S(1)}, bf16[280,1664]{1,0:T(8,128)(2,1)S(1)}) custom-call(bf16[2,4,3328]{2,1,0:T(4,128)(2,1)S(1)} %bitcast.18, bf16[2,4,3328]{2,1,0:T(4,128)(2,1)S(1)} %bitcast.19, bf16[280,1664]{1,0:T(8,128)(2,1)S(1)} %bitcast.16, ...), custom_call_target="tpu_custom_call" | custom-call | flops 2862612480 | bytes 3727360 | tf_op jit(solution)/shard_map/pallas_call | solution.py:354
  91.9 0.6 copy.12
  92.5 0.6 copy.13
  93.1 0.9 copy.14
  94.0 0.9 copy.15
Async XLA Ops:
  0.6 1.2 %copy-start = (bf16[1,1664,280]{1,2,0:T(8,128)(2,1)S(1)}, bf16[1,1664,280]{1,2,0:T(8,128)(2,1)}, u32[]{:S(2)}) copy-start(bf16[1,1664,280]{1,2,0:T(8,128)(2,1)} %param.6) | copy-start | bytes 2795524
  1.8 1.2 %copy-start.1 = (bf16[1,280,1664]{2,1,0:T(8,128)(2,1)S(1)}, bf16[1,280,1664]{2,1,0:T(8,128)(2,1)}, u32[]{:S(2)}) copy-start(bf16[1,280,1664]{2,1,0:T(8,128)(2,1)} %param.7) | copy-start | bytes 2795524
  3.0 0.8 copy-start.2
  3.8 0.8 copy-start.3

commit v2 on v1

v2 whole, which is shorter than its diff:
```python
import jax
import jax.numpy as jnp
from jax import lax
from jax.experimental import pallas as pl
from jax.experimental.pallas import tpu as pltpu
from jax.sharding import PartitionSpec as P

MESH = pl.DeviceIdType.MESH
BF, F32 = jnp.bfloat16, jnp.float32
RING = 8
HOPS = RING // 2
BLOCK = 32
PART = BLOCK // 2
EVERY = 2 * RING * BLOCK
COPIES = 114
ROOT = 0.7978845608028654
CUBE = 0.044715


def group_own(k):
    return BLOCK if k in (0, HOPS) else 2 * BLOCK


def own_at(k):
    return sum(group_own(i) for i in range(k))


def group_at(k):
    return 2 * own_at(k)


def nt(a, b):
    return lax.dot_general(a, b, (((1,), (1,)), ((), ())), preferred_element_type=F32)


def nn(a, b):
    return lax.dot_general(a, b, (((1,), (0,)), ((), ())), preferred_element_type=F32)


def tn(a, b):
    return lax.dot_general(a, b, (((0,), (0,)), ((), ())), preferred_element_type=F32)


def kernel(
    x_hbm, c_hbm, w1_hbm, w2_hbm,
    res, dx, gi_hbm, go_hbm,
    x_in, c_in, xs, xr, cs, cr, ys, yr, ds, dr, wide, X, C, w1, w2, gi, go,
    h_own, h_out, h_in, e_own, e_out, e_in, slope, act, grd,
    po, ps, pr, sp, rp, qo, qs, qr, sq, rq,
    send_sem, recv_sem, local_sem,
):
    s, t, p = (lax.axis_index(a) for a in ("section", "tensor", "dp"))
    sections = lax.axis_size("section")
    core = t % 2
    z = (t // 2) % RING
    x_hi = t // (2 * RING)
    turn = 1 - 2 * core

    def at_z(step):
        return (s, x_hi * 2 * RING + ((z + RING + step) % RING) * 2 + core, p)

    up, down, up2, down2 = at_z(turn), at_z(-turn), at_z(2 * turn), at_z(-2 * turn)
    sib = (s, t + turn, p)
    other_t = (t + 2 * RING) % (4 * RING)
    mirror = sections - 1 - s
    routes = [
        (d, x, rel, ((s, mirror)[d], (t, other_t)[x], p + rel - 2 * rel * p))
        for d in range(2)
        for x in range(2)
        for rel in range(2)
        if d + x + rel > 0
    ]
    pair = routes[0][3]
    half = w1.shape[1]

    barrier = pltpu.get_barrier_semaphore()
    peers = [up, down, up2, down2, sib] + [route[3] for route in routes]
    for peer in peers:
        pl.semaphore_signal(barrier, inc=1, device_id=peer, device_id_type=MESH)

    load_x = pltpu.make_async_copy(x_hbm, x_in, local_sem.at[4])
    load_c = pltpu.make_async_copy(c_hbm, c_in, local_sem.at[5])
    load_x.start()
    load_c.start()
    load1 = pltpu.make_async_copy(w1_hbm, w1, local_sem.at[0])
    load2 = pltpu.make_async_copy(w2_hbm, w2, local_sem.at[1])
    load1.start()
    load2.start()

    sent = []
    count = [0]

    def ticket():
        count[0] += 1
        return count[0] - 1

    def send(src, dst, device, n):
        copy = pltpu.make_async_remote_copy(
            src_ref=src, dst_ref=dst, send_sem=send_sem.at[n], recv_sem=recv_sem.at[n],
            device_id=device, device_id_type=MESH,
        )
        copy.start()
        sent.append(copy)

    def arrived(dst, device, n):
        pltpu.make_async_remote_copy(
            src_ref=dst, dst_ref=dst, send_sem=send_sem.at[n], recv_sem=recv_sem.at[n],
            device_id=device, device_id_type=MESH,
        ).wait_recv()

    for load, source, stage in ((load_x, x_in, xs), (load_c, c_in, cs)):
        load.wait()
        for d in range(2):
            for h in range(2):
                stage[d, h] = source[d, :, h * half : (h + 1) * half]
    pl.semaphore_wait(barrier, len(peers))

    def spread(land, part, piece):
        numbers = {}
        for d, x, rel, device in routes:
            if d == part:
                numbers[(x, rel)] = ticket()
                send(piece(d, x, device[2]), land.at[d, x, p], device, numbers[(x, rel)])
        return numbers

    def landed(land, part, numbers):
        for d, x, rel, device in routes:
            if d == part:
                arrived(land.at[d, x, device[2]], device, numbers[(x, rel)])

    x_spread = [spread(xr, d, lambda d, x, q: xs.at[d, q]) for d in range(2)]
    c_spread = [spread(cr, d, lambda d, x, q: cs.at[d, q]) for d in range(2)]
    xr[0, 0, p] = xs[0, p]
    cr[0, 0, p] = cs[0, p]

    def rows(ref, at, n):
        return ref.at[pl.ds(at, n)]

    pieces = [(x, q) for x in range(2) for q in range(2)]
    steps = [
        (which, k) for k in range(1, HOPS + 1) for which in range(2 if k < HOPS else 1)
    ]

    class Gather:
        def __init__(self, land, numbers, buf):
            self.land, self.numbers, self.buf = land, numbers, buf
            self.n = {(part, which, k): ticket() for which, k in steps for part in range(2)}
            self.s = [ticket() for _ in range(HOPS + 1)]

        def place(self, part, which, k):
            return rows(self.buf, group_at(k) + BLOCK * which * (k > 0) + PART * part, PART)

        def forward(self, part, which, k, to, device):
            send(self.place(part, which, k), self.place(part, which, to), device, self.n[(part, which, to)])

        def own(self, part):
            landed(self.land, part, self.numbers[part])
            for i, (x, q) in enumerate(pieces):
                wide[4 * i : 4 * i + 4, :] = self.land[part, x, q].astype(F32)
            self.buf[PART * part : PART * part + PART, :] = wide[...].astype(BF)

        def first(self, part):
            self.forward(part, 0, 0, 2, up2)
            self.forward(part, 1, 0, 2, down2)
            self.forward(part, 0, 0, 1, up)
            self.forward(part, 1, 0, 1, down)

        def here(self, part, k):
            for which, device in ((0, up), (1, down)):
                n = self.n.get((part, which, k))
                if n is not None:
                    arrived(self.place(part, which, k), device, n)

        def second(self, part):
            self.here(part, 2)
            self.forward(part, 0, 2, 4, up2)
            self.forward(part, 0, 2, 3, up)
            self.forward(part, 1, 2, 3, down)

        def hand(self, k):
            at, n = group_at(k), group_own(k)
            send(rows(self.buf, at, n), rows(self.buf, at + n, n), sib, self.s[k])

        def group(self, k):
            at, n = group_at(k), group_own(k)
            arrived(rows(self.buf, at + n, n), sib, self.s[k])

    class Inner:
        def __init__(self, gather, weight, own, out, inn):
            self.gather, self.weight = gather, weight
            self.own, self.out, self.inn = own, out, inn
            self.n = [ticket() for _ in range(HOPS + 1)]

        def make(self, k):
            self.gather.group(k)
            at, n = group_at(k), 2 * group_own(k)
            part = nt(self.gather.buf[at : at + n, :], self.weight[...])
            self.out[at : at + n, :] = part.astype(BF)
            send(rows(self.out, at, n), rows(self.inn, at, n), pair, self.n[k])
            self.own[at : at + n, :] = part

        def total(self, k):
            at, n = group_at(k), 2 * group_own(k)
            arrived(rows(self.inn, at, n), pair, self.n[k])
            return self.own[at : at + n, :] + self.inn[at : at + n, :].astype(F32)

    class Scatter:
        def __init__(self, left, weight, own, out, inn, go_on, come, base, stage, land, dest):
            self.left, self.weight = left, weight
            self.own, self.out, self.inn = own, out, inn
            self.go_on, self.come, self.base = go_on, come, base
            self.stage, self.land, self.dest = stage, land, dest
            self.s = [ticket() for _ in range(HOPS + 1)]
            self.n = {(part, which, k): ticket() for which, k in steps for part in range(2)}
            self.numbers = {}

        def make(self, k):
            at, n = group_at(k), group_own(k)
            term = nn(self.left[at : at + 2 * n, :], self.weight[...])
            to = own_at(k)
            self.out[to : to + n, :] = term[n:, :].astype(BF)
            send(rows(self.out, to, n), rows(self.inn, to, n), sib, self.s[k])
            self.own[to : to + n, :] = term[:n, :]

        def meet(self, k):
            arrived(rows(self.inn, own_at(k), group_own(k)), sib, self.s[k])

        def sums(self, part, which, k, joins):
            at = own_at(k) + BLOCK * which * (k > 0) + PART * part
            total = self.own[at : at + PART, :] + self.inn[at : at + PART, :].astype(F32)
            for side, j in joins:
                was = own_at(j) + BLOCK * side + PART * part
                arrived(rows(self.come, was, PART), sib, self.n[(part, side, j)])
                total += self.come[was : was + PART, :].astype(F32)
            return total

        def push(self, part, which, k, device, joins=()):
            at = own_at(k) + BLOCK * which + PART * part
            self.go_on[at : at + PART, :] = self.sums(part, which, k, joins).astype(BF)
            send(rows(self.go_on, at, PART), rows(self.come, at, PART), device, self.n[(part, which, k)])

        def first(self, part):
            self.push(part, 0, 4, down2)
            self.push(part, 0, 3, down)
            self.push(part, 1, 3, up)

        def near(self, part):
            self.push(part, 0, 1, down)
            self.push(part, 1, 1, up)

        def second(self, part):
            self.push(part, 1, 2, up2, ((1, 3),))
            self.push(part, 0, 2, down2, ((0, 3), (0, 4)))

        def last(self, part):
            wide[...] = self.sums(part, 0, 0, ((0, 1), (1, 1), (1, 2), (0, 2)))
            for i, (x, q) in enumerate(pieces):
                self.stage[part, x, q] = wide[4 * i : 4 * i + 4, :].astype(BF)
            self.numbers[part] = spread(self.land, part, lambda d, x, q: self.stage.at[d, x, q])
            if part == 0:
                self.land[0, 0, p] = self.stage[0, 0, p]

        def deliver(self, part):
            landed(self.land, part, self.numbers[part])
            for h in range(2):
                span = slice(h * half, (h + 1) * half)
                self.dest[part, :, span] = (
                    self.base[part, :, span].astype(F32)
                    + self.land[part, 0, h].astype(F32)
                    + self.land[part, 1, h].astype(F32)
                ).astype(BF)

    def bend(k):
        at, n = group_at(k), 2 * group_own(k)
        v = hid.total(k)
        square = v * v
        th = jnp.tanh(ROOT * (v + CUBE * (square * v)))
        gate = 0.5 * (1.0 + th)
        act[at : at + n, :] = (v * gate).astype(BF)
        slope[at : at + n, :] = gate + 0.5 * v * (1.0 - th * th) * (
            ROOT * (1.0 + 3.0 * CUBE * square)
        )

    def back(k):
        at, n = group_at(k), 2 * group_own(k)
        grd[at : at + n, :] = (err.total(k) * slope[at : at + n, :]).astype(BF)

    A, B = 0, 1
    gx, gc = Gather(xr, x_spread, X), Gather(cr, c_spread, C)
    hid = Inner(gx, w1, h_own, h_out, h_in)
    err = Inner(gc, w2, e_own, e_out, e_in)
    sc_p = Scatter(act, w2, po, ps, pr, sp, rp, x_in, ys, yr, res)
    sc_q = Scatter(grd, w1, qo, qs, qr, sq, rq, c_in, ds, dr, dx)

    gx.own(A)
    gx.first(A)
    gx.own(B)
    gx.first(B)
    gx.hand(0)
    gc.own(A)
    gc.own(B)
    load1.wait()
    load2.wait()
    gx.second(A)
    gc.first(A)
    gx.second(B)
    gc.first(B)
    gc.hand(0)
    hid.make(0)
    gx.here(A, 1)
    gx.here(B, 1)
    gx.hand(1)
    gx.hand(2)
    hid.make(1)
    hid.make(2)
    gc.second(A)
    for k in (3, 4):
        gx.here(A, k)
        gx.here(B, k)
        gx.hand(k)
    gc.second(B)
    hid.make(3)
    hid.make(4)
    gc.here(A, 1)
    gc.here(B, 1)
    gc.hand(1)
    gc.hand(2)
    err.make(0)
    bend(0)
    bend(1)
    bend(2)
    err.make(1)
    err.make(2)
    bend(3)
    bend(4)
    sc_p.make(4)
    sc_p.make(3)
    for k in (3, 4):
        gc.here(A, k)
        gc.here(B, k)
        gc.hand(k)
    sc_p.meet(4)
    sc_p.meet(3)
    sc_p.first(B)
    sc_p.first(A)
    err.make(3)
    err.make(4)
    sc_p.make(1)
    sc_p.make(2)
    sc_p.make(0)
    sc_p.meet(1)
    sc_p.near(B)
    sc_p.near(A)
    for k in range(5):
        back(k)
    sc_q.make(4)
    sc_q.make(3)
    sc_p.meet(2)
    sc_p.second(B)
    sc_p.second(A)
    sc_q.meet(4)
    sc_q.meet(3)
    sc_q.first(B)
    sc_q.first(A)
    sc_q.make(1)
    sc_q.make(2)
    sc_q.make(0)
    sc_q.meet(1)
    sc_q.near(B)
    sc_q.near(A)
    sc_q.meet(2)
    go[...] = tn(act[...], C[...]).astype(BF)
    store1 = pltpu.make_async_copy(go, go_hbm, local_sem.at[2])
    store1.start()
    sc_q.second(B)
    sc_q.second(A)
    sc_p.meet(0)
    sc_p.last(B)
    sc_p.last(A)
    gi[...] = tn(grd[...], X[...]).astype(BF)
    store2 = pltpu.make_async_copy(gi, gi_hbm, local_sem.at[3])
    store2.start()
    sc_q.meet(0)
    sc_q.last(B)
    sc_q.last(A)
    for part in (A, B):
        sc_p.deliver(part)
    for part in (A, B):
        sc_q.deliver(part)
    for copy in sent:
        copy.wait_send()
    store1.wait()
    store2.wait()


def write_out(*refs):
    n = len(refs) // 2
    copies = [
        pltpu.make_async_copy(src, dst, refs[-1].at[i]) for i, (src, dst) in enumerate(zip(refs[:n], refs[n : 2 * n]))
    ]
    for copy in copies:
        copy.start()
    for copy in copies:
        copy.wait()


def on_device(acts, cotangent, w_in, w_out):
    _, hidden, half = w_out.shape
    d_model = 2 * half
    every = EVERY
    v = pltpu.VMEM
    stage = v((2, 2, 4, half), BF)
    land = v((2, 2, 2, 4, half), BF)
    inner = [v((every, hidden), F32), v((every, hidden), BF), v((every, hidden), BF)]
    own = EVERY // 2
    outer = [v((own, half), F32)] + [v((own, half), BF)] * 4
    any_place = pl.BlockSpec(memory_space=pl.ANY)
    here = pl.BlockSpec(memory_space=pltpu.VMEM)
    made = pl.pallas_call(
        kernel,
        out_shape=(
            jax.ShapeDtypeStruct((2, 4, d_model), BF),
            jax.ShapeDtypeStruct((2, 4, d_model), BF),
            jax.ShapeDtypeStruct((hidden, half), BF),
            jax.ShapeDtypeStruct((hidden, half), BF),
        ),
        in_specs=[pl.BlockSpec(memory_space=pltpu.HBM)] * 4,
        out_specs=(here, here, any_place, any_place),
        scratch_shapes=[v((2, 4, d_model), BF)] * 2
        + [stage, land] * 2
        + [land] * 4
        + [v((16, half), F32)]
        + [v((every, half), BF)] * 2
        + [v((hidden, half), BF)] * 4
        + inner * 2
        + [v((every, hidden), F32), v((every, hidden), BF), v((every, hidden), BF)]
        + outer * 2
        + [
            pltpu.SemaphoreType.DMA((COPIES,)),
            pltpu.SemaphoreType.DMA((COPIES,)),
            pltpu.SemaphoreType.DMA((6,)),
        ],
        compiler_params=pltpu.CompilerParams(
            collective_id=0, has_side_effects=True, vmem_limit_bytes=63 * 1024 * 1024
        ),
        cost_estimate=pl.CostEstimate(
            flops=12 * every * hidden * half, bytes_accessed=8 * hidden * half, transcendentals=every * hidden
        ),
    )(acts[0], cotangent[0], jnp.swapaxes(w_in[0], 0, 1), w_out[0])
    result, d_acts, g_in, g_out = pl.pallas_call(
        write_out,
        out_shape=[jax.ShapeDtypeStruct(a.shape, a.dtype) for a in made],
        in_specs=[here] * 4,
        out_specs=[pl.BlockSpec(memory_space=pltpu.HBM)] * 4,
        scratch_shapes=[pltpu.SemaphoreType.DMA((4,))],
    )(*made)
    return (result[None], d_acts[None], jnp.swapaxes(g_in, 0, 1)[None], g_out[None])


def solution(mesh):
    placed = (
        P("section", None, ("tensor", "dp"), None),
        P("section", None, ("tensor", "dp"), None),
        P("section", "dp", "tensor"),
        P("section", "tensor", "dp"),
    )
    return jax.shard_map(on_device, mesh=mesh, in_specs=placed, out_specs=placed, check_vma=False)
```

time: 95.3 us -> 81 us (0.85)
  the two profiles are of different devices: /device:TPU:10 before, /device:TPU:8 now
where the time goes in v2:
time: 81 us; the launch traced here: 80.9 us
  Pallas kernels  80.2 us (99%)
    pallas_call x1, Pallas kernels, on_device(): pl.pallas_call(kernel, out_shape=(jax.ShapeDtypeStruct((2, 4, d_model), B...  77.4 us
    pallas_call x1, Pallas kernels, on_device(): pl.pallas_call(write_out, out_shape=[jax.ShapeDtypeStruct(a.shape, a.dtyp...  2.83 us

profile of v2, /device:TPU:8, one launch (start us, length us, event | category | flops | bytes accessed | tf_op | source)
XLA Modules:
  0.0 80.9 jit_solution(8928140025707245029)
XLA Ops:
  0.6 77.4 %shard_map.75 = (bf16[2,4,3328]{2,1,0:T(4,128)(2,1)}, bf16[2,4,3328]{2,1,0:T(4,128)(2,1)}, bf16[280,1664]{1,0:T(8,128)(2,1)}, bf16[280,1664]{1,0:T(8,128)(2,1)}) custom-call(bf16[2,4,3328]{2,1,0:T(4,128)(2,1)} %bitcast.16, bf16[2,4,3328]{2,1,0:T(4,128)(2,1)} %bitcast.17, bf16[280,1664]{1,0:T(8,128)(2,1)} %bitcast.12, bf16[280,1664]{1,0:T(8,128)(2,1)} %bitcast.13), custom_call_target="tpu_custom_call" | custom-call | flops 2862612480 | bytes 3727360 | tf_op jit(solution)/shard_map/pallas_call | solution.py:419
  78.0 2.8 %shard_map.76 = (bf16[2,4,3328]{2,1,0:T(4,128)(2,1)}, bf16[2,4,3328]{2,1,0:T(4,128)(2,1)}, bf16[280,1664]{1,0:T(8,128)(2,1)}, bf16[280,1664]{1,0:T(8,128)(2,1)}) custom-call(bf16[2,4,3328]{2,1,0:T(4,128)(2,1)} %get-tuple-element.12.refs_0_, bf16[2,4,3328]{2,1,0:T(4,128)(2,1)} %get-tuple-element.13.refs_1_, bf16[280,1664]{1,0:T(8,128)(2,1)} %get-tuple-element.14.refs_2_, ...), custom_call_target="tpu_custom_call" | custom-call | tf_op jit(solution)/shard_map/pallas_call | solution.py:450

commit v3 on v2

--- a/solution.py
+++ b/solution.py
@@ -128,8 +128,8 @@
             if d == part:
                 arrived(land.at[d, x, device[2]], device, numbers[(x, rel)])
 
-    x_spread = [spread(xr, d, lambda d, x, q: xs.at[d, q]) for d in range(2)]
-    c_spread = [spread(cr, d, lambda d, x, q: cs.at[d, q]) for d in range(2)]
+    x_spread = {d: spread(xr, d, lambda d, x, q: xs.at[d, q]) for d in (1, 0)}
+    c_spread = {d: spread(cr, d, lambda d, x, q: cs.at[d, q]) for d in (1, 0)}
     xr[0, 0, p] = xs[0, p]
     cr[0, 0, p] = cs[0, p]
 
@@ -150,32 +150,25 @@
         def place(self, part, which, k):
             return rows(self.buf, group_at(k) + BLOCK * which * (k > 0) + PART * part, PART)
 
-        def forward(self, part, which, k, to, device):
-            send(self.place(part, which, k), self.place(part, which, to), device, self.n[(part, which, to)])
+        def forward(self, part, k):
+            for which, device in ((0, up), (1, down)):
+                n = self.n.get((part, which, k + 1))
+                if n is not None:
+                    send(self.place(part, which, k), self.place(part, which, k + 1), device, n)
 
         def own(self, part):
             landed(self.land, part, self.numbers[part])
             for i, (x, q) in enumerate(pieces):
                 wide[4 * i : 4 * i + 4, :] = self.land[part, x, q].astype(F32)
             self.buf[PART * part : PART * part + PART, :] = wide[...].astype(BF)
-
-        def first(self, part):
-            self.forward(part, 0, 0, 2, up2)
-            self.forward(part, 1, 0, 2, down2)
-            self.forward(part, 0, 0, 1, up)
-            self.forward(part, 1, 0, 1, down)
-
-        def here(self, part, k):
+            self.forward(part, 0)
+
+        def step(self, part, k):
             for which, device in ((0, up), (1, down)):
                 n = self.n.get((part, which, k))
                 if n is not None:
                     arrived(self.place(part, which, k), device, n)
-
-        def second(self, part):
-            self.here(part, 2)
-            self.forward(part, 0, 2, 4, up2)
-            self.forward(part, 0, 2, 3, up)
-            self.forward(part, 1, 2, 3, down)
+            self.forward(part, k)
 
         def hand(self, k):
             at, n = group_at(k), group_own(k)
@@ -239,21 +232,27 @@
             self.go_on[at : at + PART, :] = self.sums(part, which, k, joins).astype(BF)
             send(rows(self.go_on, at, PART), rows(self.come, at, PART), device, self.n[(part, which, k)])
 
-        def first(self, part):
-            self.push(part, 0, 4, down2)
+        def far3(self, part):
             self.push(part, 0, 3, down)
             self.push(part, 1, 3, up)
 
-        def near(self, part):
-            self.push(part, 0, 1, down)
-            self.push(part, 1, 1, up)
-
-        def second(self, part):
-            self.push(part, 1, 2, up2, ((1, 3),))
-            self.push(part, 0, 2, down2, ((0, 3), (0, 4)))
+        def far4(self, part):
+            self.push(part, 0, 4, down2)
+
+        def a2(self, part):
+            self.push(part, 0, 2, down, ((0, 3), (0, 4)))
+
+        def b2(self, part):
+            self.push(part, 1, 2, up, ((1, 3),))
+
+        def a1(self, part):
+            self.push(part, 0, 1, down, ((0, 2),))
+
+        def b1(self, part):
+            self.push(part, 1, 1, up, ((1, 2),))
 
         def last(self, part):
-            wide[...] = self.sums(part, 0, 0, ((0, 1), (1, 1), (1, 2), (0, 2)))
+            wide[...] = self.sums(part, 0, 0, ((0, 1), (1, 1)))
             for i, (x, q) in enumerate(pieces):
                 self.stage[part, x, q] = wide[4 * i : 4 * i + 4, :].astype(BF)
             self.numbers[part] = spread(self.land, part, lambda d, x, q: self.stage.at[d, x, q])
@@ -293,99 +292,95 @@
     sc_q = Scatter(grd, w1, qo, qs, qr, sq, rq, c_in, ds, dr, dx)
 
     gx.own(A)
-    gx.first(A)
+    gc.own(A)
     gx.own(B)
-    gx.first(B)
     gx.hand(0)
-    gc.own(A)
-    gc.own(B)
     load1.wait()
     load2.wait()
-    gx.second(A)
-    gc.first(A)
-    gx.second(B)
-    gc.first(B)
+    gx.step(A, 1)
+    gc.step(A, 1)
+    gc.own(B)
     gc.hand(0)
-    hid.make(0)
-    gx.here(A, 1)
-    gx.here(B, 1)
-    gx.hand(1)
-    gx.hand(2)
-    hid.make(1)
-    hid.make(2)
-    gc.second(A)
-    for k in (3, 4):
-        gx.here(A, k)
-        gx.here(B, k)
+    for k in range(1, HOPS):
+        hid.make(k - 1)
+        gx.step(B, k)
         gx.hand(k)
-    gc.second(B)
+        gx.step(A, k + 1)
+        gc.step(A, k + 1)
+        gc.step(B, k)
+        gc.hand(k)
+        err.make(k - 1)
+        if k > 1:
+            bend(k - 2)
+        if k > 2:
+            back(k - 3)
     hid.make(3)
+    gx.step(B, 4)
+    gx.hand(4)
+    err.make(3)
+    bend(2)
     hid.make(4)
-    gc.here(A, 1)
-    gc.here(B, 1)
-    gc.hand(1)
-    gc.hand(2)
-    err.make(0)
-    bend(0)
-    bend(1)
-    bend(2)
-    err.make(1)
-    err.make(2)
+    gc.step(B, 4)
+    gc.hand(4)
     bend(3)
+    sc_p.make(3)
+    err.make(4)
+    back(3)
+    sc_q.make(3)
+    sc_p.meet(3)
+    sc_p.far3(B)
+    sc_p.far3(A)
+    sc_q.meet(3)
+    sc_q.far3(B)
+    sc_q.far3(A)
     bend(4)
     sc_p.make(4)
-    sc_p.make(3)
-    for k in (3, 4):
-        gc.here(A, k)
-        gc.here(B, k)
-        gc.hand(k)
+    back(4)
+    sc_q.make(4)
+    sc_p.make(2)
+    back(1)
+    back(2)
     sc_p.meet(4)
-    sc_p.meet(3)
-    sc_p.first(B)
-    sc_p.first(A)
-    err.make(3)
-    err.make(4)
-    sc_p.make(1)
-    sc_p.make(2)
-    sc_p.make(0)
-    sc_p.meet(1)
-    sc_p.near(B)
-    sc_p.near(A)
-    for k in range(5):
-        back(k)
-    sc_q.make(4)
-    sc_q.make(3)
+    sc_p.far4(B)
+    sc_p.far4(A)
+    sc_q.meet(4)
+    sc_q.far4(B)
+    sc_q.far4(A)
+    sc_q.make(2)
     sc_p.meet(2)
-    sc_p.second(B)
-    sc_p.second(A)
-    sc_q.meet(4)
-    sc_q.meet(3)
-    sc_q.first(B)
-    sc_q.first(A)
-    sc_q.make(1)
-    sc_q.make(2)
-    sc_q.make(0)
-    sc_q.meet(1)
-    sc_q.near(B)
-    sc_q.near(A)
+    sc_p.b2(B)
+    sc_p.b2(A)
     sc_q.meet(2)
+    sc_q.b2(B)
+    sc_q.b2(A)
+    for k in (1, 0):
+        sc_p.make(k)
+        sc_q.make(k)
     go[...] = tn(act[...], C[...]).astype(BF)
     store1 = pltpu.make_async_copy(go, go_hbm, local_sem.at[2])
     store1.start()
-    sc_q.second(B)
-    sc_q.second(A)
-    sc_p.meet(0)
-    sc_p.last(B)
-    sc_p.last(A)
+    for part in (B, A):
+        sc_p.a2(part)
+        sc_q.a2(part)
+    sc_p.meet(1)
+    sc_q.meet(1)
+    for part in (B, A):
+        sc_p.b1(part)
+        sc_q.b1(part)
     gi[...] = tn(grd[...], X[...]).astype(BF)
     store2 = pltpu.make_async_copy(gi, gi_hbm, local_sem.at[3])
     store2.start()
+    for part in (B, A):
+        sc_p.a1(part)
+        sc_q.a1(part)
+    sc_p.meet(0)
     sc_q.meet(0)
+    sc_p.last(B)
     sc_q.last(B)
+    sc_p.last(A)
     sc_q.last(A)
     for part in (A, B):
         sc_p.deliver(part)
-    for part in (A, B):
         sc_q.deliver(part)
     for copy in sent:
         copy.wait_send()
@@ -393,15 +388,23 @@
     store2.wait()
 
 
-def write_out(*refs):
-    n = len(refs) // 2
-    copies = [
-        pltpu.make_async_copy(src, dst, refs[-1].at[i]) for i, (src, dst) in enumerate(zip(refs[:n], refs[n : 2 * n]))
-    ]
-    for copy in copies:
-        copy.start()
-    for copy in copies:
-        copy.wait()
+def write_out(a, b, c, d, a_out, b_out, c_out, d_out, a_mid, b_mid, c_mid, d_mid, sem):
+    half = c.shape[1] // 2 // 128 * 128
+    parts = [(c, c_mid, c_out), (d, d_mid, d_out)]
+    moves = [
+        (src.at[:, span], mid.at[:, span], dst.at[:, span])
+        for src, mid, dst in parts
+        for span in (pl.ds(0, half), pl.ds(half, c.shape[1] - half))
+    ] + [(a, a_mid, a_out), (b, b_mid, b_out)]
+    loads = [pltpu.make_async_copy(m[0], m[1], sem.at[0, n]) for n, m in enumerate(moves)]
+    stores = [pltpu.make_async_copy(m[1], m[2], sem.at[1, n]) for n, m in enumerate(moves)]
+    for load in loads:
+        load.start()
+    for load, store in zip(loads, stores):
+        load.wait()
+        store.start()
+    for store in stores:
+        store.wait()
 
 
 def on_device(acts, cotangent, w_in, w_out):
@@ -450,9 +453,9 @@
     result, d_acts, g_in, g_out = pl.pallas_call(
         write_out,
         out_shape=[jax.ShapeDtypeStruct(a.shape, a.dtype) for a in made],
-        in_specs=[here] * 4,
+        in_specs=[pl.BlockSpec(memory_space=pltpu.HBM)] * 4,
         out_specs=[pl.BlockSpec(memory_space=pltpu.HBM)] * 4,
-        scratch_shapes=[pltpu.SemaphoreType.DMA((4,))],
+        scratch_shapes=[v(a.shape, a.dtype) for a in made] + [pltpu.SemaphoreType.DMA((2, 6))],
     )(*made)
     return (result[None], d_acts[None], jnp.swapaxes(g_in, 0, 1)[None], g_out[None])
 

time: 81 us -> 77.8 us (0.960)
  Pallas kernels: 80.2 us -> 77 us
    pallas_call x1, Pallas kernels: 77.4 us -> 74.6 us  [on_device(): pl.pallas_call(kernel, out_shape=(jax.ShapeDtypeStruct((2, 4, d_model), B...]
where the time goes in v3:
time: 77.8 us; the launch traced here: 77.6 us
  Pallas kernels  77 us (99%)
    pallas_call x1, Pallas kernels, on_device(): pl.pallas_call(kernel, out_shape=(jax.ShapeDtypeStruct((2, 4, d_model), B...  74.6 us
    pallas_call x1, Pallas kernels, on_device(): pl.pallas_call(write_out, out_shape=[jax.ShapeDtypeStruct(a.shape, a.dtyp...  2.38 us

profile of v3, /device:TPU:8, one launch (start us, length us, event | category | flops | bytes accessed | tf_op | source)
XLA Modules:
  0.0 77.6 jit_solution(14407718958022882739)
XLA Ops:
  0.6 74.6 %shard_map.75 = (bf16[2,4,3328]{2,1,0:T(4,128)(2,1)}, bf16[2,4,3328]{2,1,0:T(4,128)(2,1)}, bf16[280,1664]{1,0:T(8,128)(2,1)}, bf16[280,1664]{1,0:T(8,128)(2,1)}) custom-call(bf16[2,4,3328]{2,1,0:T(4,128)(2,1)} %bitcast.16, bf16[2,4,3328]{2,1,0:T(4,128)(2,1)} %bitcast.17, bf16[280,1664]{1,0:T(8,128)(2,1)} %bitcast.12, bf16[280,1664]{1,0:T(8,128)(2,1)} %bitcast.13), custom_call_target="tpu_custom_call" | custom-call | flops 2862612480 | bytes 3727360 | tf_op jit(solution)/shard_map/pallas_call | solution.py:422
  75.2 2.4 %shard_map.76 = (bf16[2,4,3328]{2,1,0:T(4,128)(2,1)}, bf16[2,4,3328]{2,1,0:T(4,128)(2,1)}, bf16[280,1664]{1,0:T(8,128)(2,1)}, bf16[280,1664]{1,0:T(8,128)(2,1)}) custom-call(bf16[2,4,3328]{2,1,0:T(4,128)(2,1)} %get-tuple-element.12.a, bf16[2,4,3328]{2,1,0:T(4,128)(2,1)} %get-tuple-element.13.b, bf16[280,1664]{1,0:T(8,128)(2,1)} %get-tuple-element.14.c, ...), custom_call_target="tpu_custom_call" | custom-call | tf_op jit(solution)/shard_map/pallas_call | solution.py:453

commit v4 on v3

--- a/solution.py
+++ b/solution.py
@@ -389,13 +389,7 @@
 
 
 def write_out(a, b, c, d, a_out, b_out, c_out, d_out, a_mid, b_mid, c_mid, d_mid, sem):
-    half = c.shape[1] // 2 // 128 * 128
-    parts = [(c, c_mid, c_out), (d, d_mid, d_out)]
-    moves = [
-        (src.at[:, span], mid.at[:, span], dst.at[:, span])
-        for src, mid, dst in parts
-        for span in (pl.ds(0, half), pl.ds(half, c.shape[1] - half))
-    ] + [(a, a_mid, a_out), (b, b_mid, b_out)]
+    moves = [(c, c_mid, c_out), (d, d_mid, d_out), (a, a_mid, a_out), (b, b_mid, b_out)]
     loads = [pltpu.make_async_copy(m[0], m[1], sem.at[0, n]) for n, m in enumerate(moves)]
     stores = [pltpu.make_async_copy(m[1], m[2], sem.at[1, n]) for n, m in enumerate(moves)]
     for load in loads:
@@ -455,7 +449,7 @@
         out_shape=[jax.ShapeDtypeStruct(a.shape, a.dtype) for a in made],
         in_specs=[pl.BlockSpec(memory_space=pltpu.HBM)] * 4,
         out_specs=[pl.BlockSpec(memory_space=pltpu.HBM)] * 4,
-        scratch_shapes=[v(a.shape, a.dtype) for a in made] + [pltpu.SemaphoreType.DMA((2, 6))],
+        scratch_shapes=[v(a.shape, a.dtype) for a in made] + [pltpu.SemaphoreType.DMA((2, 4))],
     )(*made)
     return (result[None], d_acts[None], jnp.swapaxes(g_in, 0, 1)[None], g_out[None])
 

time: 77.8 us -> 77.9 us (level)
  no operation moved by 1% of the time
where the time goes in v4:
time: 77.9 us; the launch traced here: 77.7 us
  Pallas kernels  77.1 us (99%)
    pallas_call x1, Pallas kernels, on_device(): pl.pallas_call(kernel, out_shape=(jax.ShapeDtypeStruct((2, 4, d_model), B...  74.6 us
    pallas_call x1, Pallas kernels, on_device(): pl.pallas_call(write_out, out_shape=[jax.ShapeDtypeStruct(a.shape, a.dtyp...  2.51 us

profile of v4, /device:TPU:8, one launch (start us, length us, event | category | flops | bytes accessed | tf_op | source)
XLA Modules:
  0.0 77.7 jit_solution(2161993824173235655)
XLA Ops:
  0.6 74.6 %shard_map.75 = (bf16[2,4,3328]{2,1,0:T(4,128)(2,1)}, bf16[2,4,3328]{2,1,0:T(4,128)(2,1)}, bf16[280,1664]{1,0:T(8,128)(2,1)}, bf16[280,1664]{1,0:T(8,128)(2,1)}) custom-call(bf16[2,4,3328]{2,1,0:T(4,128)(2,1)} %bitcast.16, bf16[2,4,3328]{2,1,0:T(4,128)(2,1)} %bitcast.17, bf16[280,1664]{1,0:T(8,128)(2,1)} %bitcast.12, bf16[280,1664]{1,0:T(8,128)(2,1)} %bitcast.13), custom_call_target="tpu_custom_call" | custom-call | flops 2862612480 | bytes 3727360 | tf_op jit(solution)/shard_map/pallas_call | solution.py:416
  75.2 2.5 %shard_map.76 = (bf16[2,4,3328]{2,1,0:T(4,128)(2,1)}, bf16[2,4,3328]{2,1,0:T(4,128)(2,1)}, bf16[280,1664]{1,0:T(8,128)(2,1)}, bf16[280,1664]{1,0:T(8,128)(2,1)}) custom-call(bf16[2,4,3328]{2,1,0:T(4,128)(2,1)} %get-tuple-element.12.a, bf16[2,4,3328]{2,1,0:T(4,128)(2,1)} %get-tuple-element.13.b, bf16[280,1664]{1,0:T(8,128)(2,1)} %get-tuple-element.14.c, ...), custom_call_target="tpu_custom_call" | custom-call | tf_op jit(solution)/shard_map/pallas_call | solution.py:447
